TPU v7x, 512 devices: a whole 4x8x8 slice. The times are simulated.
512 devices in a mesh: dp: 128 (over x, z_hi, y), code: 4 (over z_lo, core).
Axes of the slice: x: 4, y: 8, z: 8 (z_hi: 4, z_lo: 2; z = z_hi * 2 + z_lo), core: 2. Of those that a mesh axis runs over, the one named last changes fastest.
Arguments:
- grad_parts: bfloat16 [128, 4, 128, 6144], P('dp', 'code'), may hold values from -2.5 to 2.5
- params: float32 [4, 128, 6144], P('code', 'dp'), may hold values from -6 to 6
- moment: float32 [4, 128, 6144], P('code', 'dp'), may hold values from -2 to 2
- variance: float32 [4, 128, 6144], P('code', 'dp'), may hold values from 0.001 to 2
- holders: int32 [128, 2], P('dp'), may hold values from 0 to 3, as said below
- nodes: int32 [6], replicated, may hold values from 1 to 16, as said below
Outputs:
- new_params: float32 [4, 128, 6144], P('code', 'dp')
- new_moment: float32 [4, 128, 6144], P('code', 'dp')
- new_variance: float32 [4, 128, 6144], P('code', 'dp')
- parity_store: float32 [4, 128, 3, 6144], P('code', 'dp')
Inputs may be any that keep to these rules, and one draw needn't show every extreme that they name: `holders`: the two entries of a row are different members. All 6 nodes are different.
All inputs are finite; a program needn't handle non-finite values.
Results may differ from a plain program's by a relative error of at most 0.0003.
Values may be sent and summed in bfloat16 or wider, within the bound.
No kernel may reach another device: no remote copies, remote signals or barrier semaphores. Data moves between devices by JAX's collectives and lax.ppermute only.
A program may use at most 64 MiB of HBM per device.

v0:
```python
import jax
import jax.numpy as jnp
from jax import lax
from jax.sharding import PartitionSpec as P

beta_one = 0.9
beta_two = 0.95
learn_rate = 0.02
decay_rate = 0.1
epsilon = 1e-08
bias_one = 1.0 - 0.9**60
bias_two = 1.0 - 0.95**60


def local(grad_parts, params, moment, variance, holders, nodes):
    width = params.shape[2]
    summed = lax.psum_scatter(grad_parts.astype(jnp.float32), "dp", scatter_dimension=2, tiled=True)
    gradient = summed.reshape(params.shape)
    new_moment = beta_one * moment + (1.0 - beta_one) * gradient
    new_variance = beta_two * variance + (1.0 - beta_two) * gradient * gradient
    update = (
        new_moment / bias_one / (jnp.sqrt(new_variance / bias_two) + epsilon) + decay_rate * params
    )
    new_params = params - learn_rate * update
    states = jnp.stack([new_params[0, 0], new_moment[0, 0], new_variance[0, 0]], axis=0)
    member_count = lax.axis_size("code")
    member = lax.axis_index("code")
    node_values = nodes.astype(jnp.float32)
    coefficients = 4.0 / (node_values[:2][:, None] + node_values[2:][None, :])
    members = jnp.arange(member_count, dtype=jnp.int32)
    onehot = (holders[0][:, None] == members[None, :]).astype(jnp.float32)
    selector = (members == member).astype(jnp.float32)
    own_coef = jnp.dot(coefficients, selector, precision=lax.Precision.HIGHEST)
    weights = jnp.dot(own_coef, onehot, precision=lax.Precision.HIGHEST)
    contrib = weights[:, None, None] * states[None, :, :]
    stored = lax.psum_scatter(contrib, "code", scatter_dimension=0, tiled=True)
    parity_store = stored.reshape((1, 1, 3, width))
    return (new_params, new_moment, new_variance, parity_store)


def solution(mesh):
    return jax.shard_map(
        local,
        mesh=mesh,
        in_specs=(
            P("dp", "code", None, None),
            P("code", "dp", None),
            P("code", "dp", None),
            P("code", "dp", None),
            P("dp", None),
            P(),
        ),
        out_specs=(
            P("code", "dp", None),
            P("code", "dp", None),
            P("code", "dp", None),
            P("code", "dp", None, None),
        ),
        check_vma=False,
    )
```

profile of v0, /device:TPU:1, one launch (start us, length us, event | category | flops | bytes accessed | tf_op | source)
XLA Modules:
  0.0 848.3 jit_solution(2181223617590567474)
XLA Ops:
  7.2 0.0 copy-start.6
  7.2 0.0 copy-start.7
  7.2 0.0 copy-start.3
  7.2 0.0 copy-start.4
  7.2 0.0 copy-start.5
  7.2 0.0 all-reduce.5.cloned.1.call-start
  7.3 680.2 %all-reduce.6 = f32[1,1,128,6144]{3,2,1,0:T(8,128)S(1)} all-reduce(bf16[1,1,128,6144]{3,2,1,0:T(8,128)(2,1)} %param.6), channel_id=2, replica_groups=mesh['dp'=128,'code'=4] {'dp'}, use_global_device_ids=true, to_apply=%region_0.0.clone | all-reduce | flops 786432 | bytes 4718592
  687.5 0.0 copy-done.6
  687.5 0.1 slice.7
  687.6 1.3 dynamic-slice
  688.9 0.2 convolution_bitcast_fusion.1
  689.1 0.0 copy-done.7
  689.1 0.2 convolution_bitcast_fusion
  689.3 0.0 copy-done.3
  689.3 0.0 copy-done.4
  689.3 0.0 copy-done.5
  689.3 0.8 multiply_subtract_fusion
  690.1 0.0 copy-start
  690.1 0.0 copy-start.1
  690.1 0.0 copy-start.2
  690.1 0.1 pad_maximum_fusion
  690.2 0.9 broadcast_multiply_fusion
  691.1 0.0 all-reduce.5.cloned.1.call-update
  691.1 1.3 dynamic-slice.2
  692.4 146.7 %all-reduce.5.cloned.1.call-done = f32[4,3,6144]{2,1,0:T(4,128)} async-done(((f32[4,3,6144]{2,1,0:T(4,128)}), f32[4,3,6144]{2,1,0:T(4,128)}) %all-reduce.5.cloned.1.call-update) | async-done | bytes 294928
  839.1 1.6 dynamic-slice_bitcast_fusion
  840.7 0.7 copy.10
  841.4 0.0 copy-done
  841.4 0.0 copy-done.1
  841.4 0.0 copy-done.2
  (1 shorter events, 0.0 us)
Async XLA Ops:
  7.2 680.3 %copy-start.6 = (s32[6]{0:T(128)S(1)}, s32[6]{0:T(128)}, u32[]{:S(2)}) copy-start(s32[6]{0:T(128)} %param.11) | copy-start | bytes 76
  7.2 681.9 %copy-start.7 = (s32[1,2]{1,0:T(1,128)S(1)}, s32[1,2]{1,0:T(1,128)}, u32[]{:S(2)}) copy-start(s32[1,2]{1,0:T(1,128)} %param.10) | copy-start | bytes 28
  7.2 682.1 %copy-start.3 = (f32[1,1,6144]{2,1,0:T(1,128)S(1)}, f32[1,1,6144]{2,1,0:T(1,128)}, u32[]{:S(2)}) copy-start(f32[1,1,6144]{2,1,0:T(1,128)} %param.7) | copy-start | bytes 73732
  7.2 682.1 %copy-start.4 = (f32[1,1,6144]{2,1,0:T(1,128)S(1)}, f32[1,1,6144]{2,1,0:T(1,128)}, u32[]{:S(2)}) copy-start(f32[1,1,6144]{2,1,0:T(1,128)} %param.8) | copy-start | bytes 73732
  7.2 682.1 %copy-start.5 = (f32[1,1,6144]{2,1,0:T(1,128)S(1)}, f32[1,1,6144]{2,1,0:T(1,128)}, u32[]{:S(2)}) copy-start(f32[1,1,6144]{2,1,0:T(1,128)} %param.9) | copy-start | bytes 73732
  7.2 831.9 %all-reduce.5.cloned.1.call-start = ((), (), s32[]{:S(2)}) async-start(), calls=%async_computation | async-start | bytes 786432
  690.1 151.3 %copy-start = (f32[1,1,6144]{2,1,0:T(1,128)}, f32[1,1,6144]{2,1,0:T(1,128)S(1)}, u32[]{:S(2)}) copy-start(f32[1,1,6144]{2,1,0:T(1,128)S(1)} %get-tuple-element.8) | copy-start | bytes 73732
  690.1 151.3 %copy-start.1 = (f32[1,1,6144]{2,1,0:T(1,128)}, f32[1,1,6144]{2,1,0:T(1,128)S(1)}, u32[]{:S(2)}) copy-start(f32[1,1,6144]{2,1,0:T(1,128)S(1)} %get-tuple-element.9) | copy-start | bytes 73732
  690.1 151.3 %copy-start.2 = (f32[1,1,6144]{2,1,0:T(1,128)}, f32[1,1,6144]{2,1,0:T(1,128)S(1)}, u32[]{:S(2)}) copy-start(f32[1,1,6144]{2,1,0:T(1,128)S(1)} %get-tuple-element.10) | copy-start | bytes 73732
Sparse Core Ops, SparseCore 0:
  691.3 147.8 all-reduce.4
where the time goes:
time: 849 us; the launch traced here: 848 us
  blocking collectives  680 us (80%)
  waiting for transfers between devices  147 us (17%)
  between operations  14.2 us (2%)
    unnamed x1, blocking collectives  680 us
    unnamed x2, waiting for transfers between devices  147 us
  transfers between devices with their start and end apart: 1, of which 1 were waited for; matrix products, arithmetic and copies ran while one was open for 0% of the time, Pallas kernels for 0%

commit v1 on v0

v1 whole, which is shorter than its diff:
```python
import jax
import jax.numpy as jnp
from jax import lax
from jax.experimental import pallas as pl
from jax.experimental.pallas import tpu as pltpu
from jax.sharding import Mesh, PartitionSpec as P

beta_one = 0.9
beta_two = 0.95
learn_rate = 0.02
decay_rate = 0.1
epsilon = 1e-08
bias_one = 1.0 - 0.9**60
bias_two = 1.0 - 0.95**60

DP = ("x", "zh", "yh", "yl")
LANES = 128


def parity_kernel(holders_ref, nodes_ref, states_ref, out_ref):
    member = lax.axis_index("code")
    own = [jnp.where(holders_ref[0, j] == member, 1.0, 0.0) for j in range(2)]
    total = None
    for i in range(states_ref.shape[0]):
        data_node = nodes_ref[2 + i].astype(jnp.float32)
        weight = jnp.zeros((1, LANES), jnp.float32)
        for j in range(2):
            node = nodes_ref[j].astype(jnp.float32)
            weight += own[j] * (4.0 / jnp.full((1, LANES), node + data_node, jnp.float32))
        term = weight * states_ref[i]
        total = term if total is None else total + term
    out_ref[...] = total


def local(grad_parts, params, moment, variance, holders, nodes):
    width = params.shape[2]
    rows = width // LANES
    x, pair = lax.axis_size("x"), lax.axis_size("yl")
    rest = lax.axis_size("zh") * lax.axis_size("yh")

    parts = grad_parts.reshape(x, rest, pair, rows, LANES).transpose(0, 2, 1, 3, 4)
    parts = parts.reshape(x * pair, rest, rows, LANES)
    parts = lax.all_to_all(parts, ("x", "yl"), 0, 0, tiled=True)
    summed = jnp.sum(parts.astype(jnp.float32), axis=0)
    summed = lax.all_to_all(summed, ("zh", "yh"), 0, 0, tiled=True)
    gradient = jnp.sum(summed, axis=0)

    params = params.reshape(rows, LANES)
    new_moment = beta_one * moment.reshape(rows, LANES) + (1.0 - beta_one) * gradient
    new_variance = (
        beta_two * variance.reshape(rows, LANES) + (1.0 - beta_two) * gradient * gradient
    )
    update = (
        new_moment / bias_one / (jnp.sqrt(new_variance / bias_two) + epsilon) + decay_rate * params
    )
    new_params = params - learn_rate * update

    states = jnp.concatenate([new_params, new_moment, new_variance], axis=0)
    states = lax.all_gather(states, "code", axis=0, tiled=False)
    parity = pl.pallas_call(
        parity_kernel,
        out_shape=jax.ShapeDtypeStruct((3 * rows, LANES), jnp.float32),
        in_specs=[pl.BlockSpec(memory_space=pltpu.SMEM)] * 2
        + [pl.BlockSpec(memory_space=pltpu.VMEM)],
        out_specs=pl.BlockSpec(memory_space=pltpu.VMEM),
    )(holders, nodes, states)
    return (
        new_params.reshape(1, 1, width),
        new_moment.reshape(1, 1, width),
        new_variance.reshape(1, 1, width),
        parity.reshape(1, 1, 3, width),
    )


def solution(mesh):
    fine = Mesh(mesh.devices.reshape(4, 4, 4, 2, mesh.shape["code"]), DP + ("code",))
    return jax.shard_map(
        local,
        mesh=fine,
        in_specs=(
            P(DP, "code", None, None),
            P("code", DP, None),
            P("code", DP, None),
            P("code", DP, None),
            P(DP, None),
            P(),
        ),
        out_specs=(
            P("code", DP, None),
            P("code", DP, None),
            P("code", DP, None),
            P("code", DP, None, None),
        ),
        check_vma=False,
    )
```

time: 849 us -> 70.4 us (0.08)
  blocking collectives: 680 us -> 64.8 us
  waiting for transfers between devices: 147 us -> 0 us
  between operations: 14.2 us -> 0.69 us
    unnamed x1 -> x0, blocking collectives: 680 us -> none
    unnamed x2 -> x0, waiting for transfers between devices: 147 us -> none
    all_to_all x0 -> x2, blocking collectives: none -> 55.3 us  [the longest x1 31.9 us: local(): summed = lax.all_to_all(summed, ('zh', 'yh'), 0, 0, tiled=True)]
    all_gather x0 -> x1, blocking collectives: none -> 9.57 us  [local(): states = lax.all_gather(states, 'code', axis=0, tiled=False)]
  transfers between devices with their start and end apart: 1 -> 0, of which waited for: 1 -> 0; matrix products, arithmetic and copies ran while one was open for 0% -> 0% of each run, Pallas kernels for 0% -> 0%
where the time goes in v1:
time: 70.4 us; the launch traced here: 70.1 us
  blocking collectives  64.8 us (92%)
  local copies, waits for them, and re-layouts  1.87 us (3%)
  Pallas kernels  1.64 us (2%)
  other arithmetic  1.09 us (2%)
    all_to_all x1, blocking collectives, local(): summed = lax.all_to_all(summed, ('zh', 'yh'), 0, 0, tiled=True)  31.9 us
    all_to_all x1, blocking collectives, local(): parts = lax.all_to_all(parts, ('x', 'yl'), 0, 0, tiled=True)  23.4 us
    all_gather x1, blocking collectives, local(): states = lax.all_gather(states, 'code', axis=0, tiled=False)  9.57 us
    unnamed x7, local copies, waits for them, and re-layouts  1.76 us
    pallas_call x1, Pallas kernels, local(): pl.pallas_call(parity_kernel, out_shape=jax.ShapeDtypeStruct((3 * rows, L...  1.64 us

profile of v1, /device:TPU:1, one launch (start us, length us, event | category | flops | bytes accessed | tf_op | source)
XLA Modules:
  0.0 70.1 jit_solution(5988637903375256104)
XLA Ops:
  0.6 1.8 %copy.16 = bf16[16,8,48,128]{3,2,1,0:T(8,128)(2,1)S(1)} copy(bf16[16,8,48,128]{3,1,2,0:T(8,128)(2,1)} %bitcast.16) | data formatting | bytes 3145728
  2.4 0.1 copy.14
  2.5 23.4 %all_to_all.10 = bf16[8,16,48,128]{3,2,1,0:T(8,128)(2,1)S(1)} all-to-all(bf16[8,16,48,128]{3,2,1,0:T(8,128)(2,1)S(1)} %bitcast.14), channel_id=1, replica_groups=mesh['x'=4,'zh'=4,'yh'=4,'yl'=2,'code'=4] {'x','yl'}, dimensions={0} | all-to-all | bytes 3145728 | tf_op jit(solution)/shard_map/all_to_all | solution.py:43
  25.9 0.0 copy-start
  25.9 0.0 copy-start.1
  25.9 0.0 copy-start.2
  25.9 0.2 convert_reduce_fusion
  26.2 31.9 %all_to_all.11 = f32[16,48,128]{2,1,0:T(8,128)S(1)} all-to-all(f32[16,48,128]{2,1,0:T(8,128)S(1)} %convert_reduce_fusion), channel_id=1, replica_groups=mesh['x'=4,'zh'=4,'yh'=4,'yl'=2,'code'=4] {'zh','yh'}, dimensions={0} | all-to-all | bytes 786432 | tf_op jit(solution)/shard_map/all_to_all | solution.py:45
  58.0 0.0 copy-done
  58.1 0.0 copy-done.1
  58.1 0.0 copy-done.2
  58.1 0.8 %multiply_subtract_fusion.1 = (f32[1,1,6144]{2,1,0:T(1,128)}, f32[1,1,6144]{2,1,0:T(1,128)}, f32[1,1,6144]{2,1,0:T(1,128)}, f32[1,1,6144]{2,1,0:T(1,128)S(1)}, f32[1,1,6144]{2,1,0:T(1,128)S(1)}) fusion(f32[1,1,6144]{2,1,0:T(1,128)S(1)} %copy-done, f32[1,1,6144]{2,1,0:T(1,128)S(1)} %bitcast.18, f32[1,1,6144]{2,1,0:T(1,128)S(1)} %copy-done.1, ...), kind=kLoop, calls=%fused_computation.8 | loop fusion | flops 92160 | bytes 221184 | tf_op jit(solution)/shard_map/sub | solution.py:56
  58.9 9.6 %all-gather = f32[576,128]{1,0:T(8,128)} all-gather(f32[144,128]{1,0:T(8,128)S(1)} %pad_maximum_fusion), channel_id=2, replica_groups=mesh['x'=4,'zh'=4,'yh'=4,'yl'=2,'code'=4] {'code'}, dimensions={0}, use_global_device_ids=true | all-gather | bytes 368640 | tf_op jit(solution)/shard_map/all_gather | solution.py:59
  68.5 1.6 %shard_map.93 = f32[144,128]{1,0:T(8,128)} custom-call(s32[1,2]{1,0:T(1,128)} %holders_ref.1, s32[6]{0:T(128)} %nodes_ref.1, f32[4,144,128]{2,1,0:T(8,128)} %bitcast.17), custom_call_target="tpu_custom_call" | custom-call | tf_op jit(solution)/shard_map/pallas_call | solution.py:60
  (3 shorter events, 0.1 us)
Async XLA Ops:
  25.9 32.1 %copy-start = (f32[1,1,6144]{2,1,0:T(1,128)S(1)}, f32[1,1,6144]{2,1,0:T(1,128)}, u32[]{:S(2)}) copy-start(f32[1,1,6144]{2,1,0:T(1,128)} %param.7) | copy-start | bytes 73732
  25.9 32.1 %copy-start.1 = (f32[1,1,6144]{2,1,0:T(1,128)S(1)}, f32[1,1,6144]{2,1,0:T(1,128)}, u32[]{:S(2)}) copy-start(f32[1,1,6144]{2,1,0:T(1,128)} %param.8) | copy-start | bytes 73732
  25.9 32.1 %copy-start.2 = (f32[1,1,6144]{2,1,0:T(1,128)S(1)}, f32[1,1,6144]{2,1,0:T(1,128)}, u32[]{:S(2)}) copy-start(f32[1,1,6144]{2,1,0:T(1,128)} %param.9) | copy-start | bytes 73732

commit v2 on v1

v2 whole, which is shorter than its diff:
```python
import jax
import jax.numpy as jnp
from jax import lax
from jax.experimental import pallas as pl
from jax.experimental.pallas import tpu as pltpu
from jax.sharding import Mesh, PartitionSpec as P

beta_one = 0.9
beta_two = 0.95
learn_rate = 0.02
decay_rate = 0.1
epsilon = 1e-08
bias_one = 1.0 - 0.9**60
bias_two = 1.0 - 0.95**60

X, Z, Y = 4, 4, 8
DP = ("xh", "xl", "zh", "yh", "yl")
CODE = ("zl", "core")
LANES = 128
SCALE = 4096.0


def pairs(size, shifted):
    return [((2 * k + 2 * shifted) % size, 2 * k + 1) for k in range(size // 2)]


def near_groups():
    groups = []
    for z in range(Z):
        for zl in range(2):
            for core in range(2):
                for along_x in pairs(X, core):
                    for along_y in pairs(Y, core):
                        groups.append(
                            [
                                (((x * Z + z) * Y + y) * 2 + zl) * 2 + core
                                for x in along_x
                                for y in along_y
                            ]
                        )
    return groups


def finish_kernel(
    holders_ref, nodes_ref, own_ref, states_ref, params_ref, moment_ref, variance_ref, parity_ref,
    total_ref, sems,
):
    rows = params_ref.shape[0]
    copies = [
        pltpu.make_async_copy(own_ref.at[pl.ds(rows * k, rows)], out_ref, sems.at[k])
        for k, out_ref in enumerate((params_ref, moment_ref, variance_ref))
    ]
    for copy in copies:
        copy.start()
    member = lax.axis_index(CODE)
    held = [jnp.where(holders_ref[0, j] == member, 1.0, 0.0) for j in range(2)]
    total = None
    for i in range(states_ref.shape[0]):
        data_node = nodes_ref[2 + i].astype(jnp.float32)
        weight = jnp.zeros((1, LANES), jnp.float32)
        for j in range(2):
            node = nodes_ref[j].astype(jnp.float32)
            weight += held[j] * (4.0 / jnp.full((1, LANES), node + data_node, jnp.float32))
        term = weight * states_ref[i]
        total = term if total is None else total + term
    total_ref[...] = total
    copies.append(pltpu.make_async_copy(total_ref, parity_ref, sems.at[3]))
    copies[3].start()
    for copy in copies:
        copy.wait()


def local(grad_parts, params, moment, variance, holders, nodes):
    width = params.shape[2]
    rows = width // LANES

    parts = grad_parts.reshape(X // 2, 2, Z, Y // 2, 2, rows, LANES)
    parts = parts.transpose(1, 4, 0, 2, 3, 5, 6).reshape(4, X * Z * Y // 4, rows, LANES)
    parts = lax.all_to_all(
        parts, DP + CODE, 0, 0, tiled=True, axis_index_groups=near_groups()
    )
    summed = jnp.sum(parts.astype(jnp.float32), axis=0)
    summed = (summed * SCALE).astype(jnp.float16)
    summed = lax.all_to_all(summed, ("xh", "zh", "yh"), 0, 0, tiled=True)
    gradient = jnp.sum(summed.astype(jnp.float32), axis=0) * (1.0 / SCALE)

    gradient, params, moment, variance = lax.optimization_barrier(
        (
            gradient,
            params.reshape(rows, LANES),
            moment.reshape(rows, LANES),
            variance.reshape(rows, LANES),
        )
    )
    new_moment = beta_one * moment + (1.0 - beta_one) * gradient
    new_variance = beta_two * variance + (1.0 - beta_two) * gradient * gradient
    update = (
        new_moment / bias_one / (jnp.sqrt(new_variance / bias_two) + epsilon) + decay_rate * params
    )
    new_params = params - learn_rate * update

    own = jnp.concatenate([new_params, new_moment, new_variance], axis=0)
    states = lax.all_gather(own, CODE, axis=0, tiled=False)
    state = jax.ShapeDtypeStruct((rows, LANES), jnp.float32)
    new_params, new_moment, new_variance, parity = pl.pallas_call(
        finish_kernel,
        out_shape=(state, state, state, jax.ShapeDtypeStruct((3 * rows, LANES), jnp.float32)),
        in_specs=[pl.BlockSpec(memory_space=pltpu.SMEM)] * 2
        + [pl.BlockSpec(memory_space=pltpu.VMEM)] * 2,
        out_specs=(pl.BlockSpec(memory_space=pl.ANY),) * 4,
        scratch_shapes=[
            pltpu.VMEM((3 * rows, LANES), jnp.float32),
            pltpu.SemaphoreType.DMA((4,)),
        ],
        compiler_params=pltpu.CompilerParams(vmem_limit_bytes=4 << 20),
    )(holders, nodes, own, states)
    return (
        new_params.reshape(1, 1, width),
        new_moment.reshape(1, 1, width),
        new_variance.reshape(1, 1, width),
        parity.reshape(1, 1, 3, width),
    )


def solution(mesh):
    fine = Mesh(mesh.devices.reshape(X // 2, 2, Z, Y // 2, 2, 2, 2), DP + CODE)
    return jax.shard_map(
        local,
        mesh=fine,
        in_specs=(
            P(DP, CODE, None, None),
            P(CODE, DP, None),
            P(CODE, DP, None),
            P(CODE, DP, None),
            P(DP, None),
            P(),
        ),
        out_specs=(
            P(CODE, DP, None),
            P(CODE, DP, None),
            P(CODE, DP, None),
            P(CODE, DP, None, None),
        ),
        check_vma=False,
    )
```

time: 70.4 us -> 64.1 us (0.911)
  blocking collectives: 64.8 us -> 59.4 us
    all_to_all x2, blocking collectives: 55.3 us -> 52.5 us  [the longest x1 31.2 us: local(): summed = lax.all_to_all(summed, ('xh', 'zh', 'yh'), 0, 0, tiled=True)]
    all_gather x1, blocking collectives: 9.57 us -> 6.99 us  [local(): states = lax.all_gather(own, CODE, axis=0, tiled=False)]
    sub x2 -> x1, other arithmetic: 0.84 us -> 0.04 us  [local(): new_params = params - learn_rate * update]
    unnamed x7 -> x11, local copies, waits for them, and re-layouts: 1.76 us -> 1.78 us
where the time goes in v2:
time: 64.1 us; the launch traced here: 63.8 us
  blocking collectives  59.4 us (93%)
  local copies, waits for them, and re-layouts  1.97 us (3%)
  Pallas kernels  1.25 us (2%)
  between operations  0.74 us (1%)
    all_to_all x1, blocking collectives, local(): summed = lax.all_to_all(summed, ('xh', 'zh', 'yh'), 0, 0, tiled=True)  31.2 us
    all_to_all x1, blocking collectives, local(): lax.all_to_all(parts, DP + CODE, 0, 0, tiled=True, axis_index_groups=near...  21.3 us
    all_gather x1, blocking collectives, local(): states = lax.all_gather(own, CODE, axis=0, tiled=False)  6.99 us
    unnamed x11, local copies, waits for them, and re-layouts  1.78 us

profile of v2, /device:TPU:1, one launch (start us, length us, event | category | flops | bytes accessed | tf_op | source)
XLA Modules:
  0.0 63.8 jit_solution(16553727387311705614)
XLA Ops:
  0.6 1.8 %copy.16 = bf16[16,8,48,128]{3,2,1,0:T(8,128)(2,1)S(1)} copy(bf16[16,8,48,128]{3,1,2,0:T(8,128)(2,1)} %bitcast.19) | data formatting | bytes 3145728
  2.4 0.2 copy.14
  2.6 21.3 %all_to_all.10 = bf16[4,32,48,128]{3,2,1,0:T(8,128)(2,1)S(1)} all-to-all(bf16[4,32,48,128]{3,2,1,0:T(8,128)(2,1)S(1)} %bitcast.17), channel_id=1, replica_groups={{0,4,128,132},{8,12,136,140},{16,20,144,148},{24,28,152,156},{256,260,3..., dimensions={0} | all-to-all | bytes 3145728 | tf_op jit(solution)/shard_map/all_to_all | solution.py:79
  23.9 0.2 convert_reduce_fusion
  24.1 0.0 copy-start.2
  24.1 0.0 copy-start.3
  24.1 0.0 copy-start.4
  24.2 0.0 copy-start
  24.2 0.0 copy-start.1
  24.2 0.1 multiply_convert_fusion
  24.3 31.2 %all_to_all.11 = f16[32,48,128]{2,1,0:T(8,128)(2,1)S(1)} all-to-all(f16[32,48,128]{2,1,0:T(8,128)(2,1)S(1)} %multiply_convert_fusion), channel_id=1, replica_groups=mesh['xh'=2,'xl'=2,'zh'=4,'yh'=4,'yl'=2,'zl'=2,'core'=2] {'xh','zh','yh'}, dimensions={0} | all-to-all | bytes 786432 | tf_op jit(solution)/shard_map/all_to_all | solution.py:84
  55.4 0.1 convert_reduce_fusion.1
  55.5 0.0 copy-done.2
  55.5 0.0 copy-done.3
  55.5 0.0 copy-done.4
  55.6 7.0 %all-gather = f32[576,128]{1,0:T(8,128)S(1)} all-gather(f32[144,128]{1,0:T(8,128)S(1)} %pad_maximum_fusion.own_ref), channel_id=2, replica_groups=mesh['xh'=2,'xl'=2,'zh'=4,'yh'=4,'yl'=2,'zl'=2,'core'=2] {'zl','core'}, dimensions={0}, use_global_device_ids=true | all-gather | bytes 368640 | tf_op jit(solution)/shard_map/all_gather | solution.py:103
  62.6 0.0 copy-done
  62.6 0.0 copy-done.1
  62.6 1.3 %shard_map.93 = (f32[48,128]{1,0:T(8,128)}, f32[48,128]{1,0:T(8,128)}, f32[48,128]{1,0:T(8,128)}, f32[144,128]{1,0:T(8,128)}) custom-call(s32[1,2]{1,0:T(1,128)S(1)} %copy-done, s32[6]{0:T(128)S(1)} %copy-done.1, f32[144,128]{1,0:T(8,128)S(1)} %pad_maximum_fusion.own_ref, f32[4,144,128]{2,1,0:T(8,128)S(1)} %bitcast.16), custom_call_target="tpu_custom_call" | custom-call | tf_op jit(solution)/shard_map/pallas_call | solution.py:105
  (3 shorter events, 0.1 us)
Async XLA Ops:
  24.1 31.4 %copy-start.2 = (f32[1,1,6144]{2,1,0:T(1,128)S(1)}, f32[1,1,6144]{2,1,0:T(1,128)}, u32[]{:S(2)}) copy-start(f32[1,1,6144]{2,1,0:T(1,128)} %param.7) | copy-start | bytes 73732
  24.1 31.4 %copy-start.3 = (f32[1,1,6144]{2,1,0:T(1,128)S(1)}, f32[1,1,6144]{2,1,0:T(1,128)}, u32[]{:S(2)}) copy-start(f32[1,1,6144]{2,1,0:T(1,128)} %param.8) | copy-start | bytes 73732
  24.1 31.4 %copy-start.4 = (f32[1,1,6144]{2,1,0:T(1,128)S(1)}, f32[1,1,6144]{2,1,0:T(1,128)}, u32[]{:S(2)}) copy-start(f32[1,1,6144]{2,1,0:T(1,128)} %param.9) | copy-start | bytes 73732
  24.2 38.4 %copy-start = (s32[1,2]{1,0:T(1,128)S(1)}, s32[1,2]{1,0:T(1,128)}, u32[]{:S(2)}) copy-start(s32[1,2]{1,0:T(1,128)} %holders_ref.1) | copy-start | bytes 28
  24.2 38.4 %copy-start.1 = (s32[6]{0:T(128)S(1)}, s32[6]{0:T(128)}, u32[]{:S(2)}) copy-start(s32[6]{0:T(128)} %nodes_ref.1) | copy-start | bytes 76

commit v3 on v2

--- a/solution.py
+++ b/solution.py
@@ -41,6 +41,23 @@
     return groups
 
 
+def far_groups():
+    groups = []
+    for xl in range(2):
+        for yl in range(2):
+            for zl in range(2):
+                for core in range(2):
+                    groups.append(
+                        [
+                            (((x * Z + z) * Y + y) * 2 + zl) * 2 + core
+                            for x in (2 + xl, xl)
+                            for z in reversed(range(Z))
+                            for y in (4 + yl, 6 + yl, yl, 2 + yl)
+                        ]
+                    )
+    return groups
+
+
 def finish_kernel(
     holders_ref, nodes_ref, own_ref, states_ref, params_ref, moment_ref, variance_ref, parity_ref,
     total_ref, sems,
@@ -53,14 +70,14 @@
     for copy in copies:
         copy.start()
     member = lax.axis_index(CODE)
-    held = [jnp.where(holders_ref[0, j] == member, 1.0, 0.0) for j in range(2)]
+    holders = holders_ref[...]
+    nodes = nodes_ref[...].astype(jnp.float32)
     total = None
     for i in range(states_ref.shape[0]):
-        data_node = nodes_ref[2 + i].astype(jnp.float32)
-        weight = jnp.zeros((1, LANES), jnp.float32)
+        weight = jnp.zeros((1, 1), jnp.float32)
         for j in range(2):
-            node = nodes_ref[j].astype(jnp.float32)
-            weight += held[j] * (4.0 / jnp.full((1, LANES), node + data_node, jnp.float32))
+            held = jnp.where(holders[:, j : j + 1] == member, 4.0, 0.0)
+            weight += held / (nodes[:, j : j + 1] + nodes[:, 2 + i : 3 + i])
         term = weight * states_ref[i]
         total = term if total is None else total + term
     total_ref[...] = total
@@ -81,7 +98,11 @@
     )
     summed = jnp.sum(parts.astype(jnp.float32), axis=0)
     summed = (summed * SCALE).astype(jnp.float16)
-    summed = lax.all_to_all(summed, ("xh", "zh", "yh"), 0, 0, tiled=True)
+    pieces = summed.reshape(X // 2, Z, 2, Y // 4, rows, LANES)
+    pieces = lax.rev(pieces, (0, 1, 2)).reshape(summed.shape)
+    summed = lax.all_to_all(
+        pieces, DP + CODE, 0, 0, tiled=True, axis_index_groups=far_groups()
+    )
     gradient = jnp.sum(summed.astype(jnp.float32), axis=0) * (1.0 / SCALE)
 
     gradient, params, moment, variance = lax.optimization_barrier(
@@ -105,15 +126,14 @@
     new_params, new_moment, new_variance, parity = pl.pallas_call(
         finish_kernel,
         out_shape=(state, state, state, jax.ShapeDtypeStruct((3 * rows, LANES), jnp.float32)),
-        in_specs=[pl.BlockSpec(memory_space=pltpu.SMEM)] * 2
-        + [pl.BlockSpec(memory_space=pltpu.VMEM)] * 2,
+        in_specs=[pl.BlockSpec(memory_space=pltpu.VMEM)] * 4,
         out_specs=(pl.BlockSpec(memory_space=pl.ANY),) * 4,
         scratch_shapes=[
             pltpu.VMEM((3 * rows, LANES), jnp.float32),
             pltpu.SemaphoreType.DMA((4,)),
         ],
         compiler_params=pltpu.CompilerParams(vmem_limit_bytes=4 << 20),
-    )(holders, nodes, own, states)
+    )(holders, nodes.reshape(1, -1), own, states)
     return (
         new_params.reshape(1, 1, width),
         new_moment.reshape(1, 1, width),

time: 64.1 us -> 58.7 us (0.916)
  blocking collectives: 59.4 us -> 54.3 us
    all_to_all x1, blocking collectives: 31.2 us -> 27 us  [local(): lax.all_to_all(pieces, DP + CODE, 0, 0, tiled=True, axis_index_groups=far...]
    all_gather x1, blocking collectives: 6.99 us -> 6.04 us  [local(): states = lax.all_gather(own, CODE, axis=0, tiled=False)]
where the time goes in v3:
time: 58.7 us; the launch traced here: 58.4 us
  blocking collectives  54.3 us (93%)
  local copies, waits for them, and re-layouts  2.05 us (3%)
  Pallas kernels  0.9 us (2%)
  between operations  0.75 us (1%)
    all_to_all x1, blocking collectives, local(): lax.all_to_all(pieces, DP + CODE, 0, 0, tiled=True, axis_index_groups=far...  27 us
    all_to_all x1, blocking collectives, local(): lax.all_to_all(parts, DP + CODE, 0, 0, tiled=True, axis_index_groups=near...  21.3 us
    all_gather x1, blocking collectives, local(): states = lax.all_gather(own, CODE, axis=0, tiled=False)  6.04 us
    unnamed x11, local copies, waits for them, and re-layouts  1.78 us

profile of v3, /device:TPU:1, one launch (start us, length us, event | category | flops | bytes accessed | tf_op | source)
XLA Modules:
  0.0 58.4 jit_solution(10412769687779864656)
XLA Ops:
  0.6 1.8 %copy.16 = bf16[16,8,48,128]{3,2,1,0:T(8,128)(2,1)S(1)} copy(bf16[16,8,48,128]{3,1,2,0:T(8,128)(2,1)} %bitcast.23) | data formatting | bytes 3145728
  2.4 0.2 copy.14
  2.6 21.3 %all_to_all.10 = bf16[4,32,48,128]{3,2,1,0:T(8,128)(2,1)S(1)} all-to-all(bf16[4,32,48,128]{3,2,1,0:T(8,128)(2,1)S(1)} %bitcast.21), channel_id=1, replica_groups={{0,4,128,132},{8,12,136,140},{16,20,144,148},{24,28,152,156},{256,260,3..., dimensions={0} | all-to-all | bytes 3145728 | tf_op jit(solution)/shard_map/all_to_all | solution.py:96
  23.9 0.2 convert_reduce_fusion
  24.1 0.0 copy-start.2
  24.1 0.0 copy-start.3
  24.1 0.0 copy-start.4
  24.2 0.1 multiply_convert_fusion
  24.2 0.0 copy-start
  24.3 0.0 copy-start.1
  24.3 0.1 rev.3
  24.4 27.0 %all_to_all.11 = f16[32,48,128]{2,1,0:T(8,128)(2,1)S(1)} all-to-all(f16[32,48,128]{2,1,0:T(8,128)(2,1)S(1)} %bitcast.24), channel_id=1, replica_groups={{368,376,352,360,336,344,320,328,304,312,288,296,272,280,256,264,112,12..., dimensions={0} | all-to-all | bytes 786432 | tf_op jit(solution)/shard_map/all_to_all | solution.py:103
  51.3 0.1 convert_reduce_fusion.1
  51.4 0.0 copy-done.2
  51.4 0.0 copy-done.3
  51.4 0.0 copy-done.4
  51.5 6.0 %all-gather = f32[576,128]{1,0:T(8,128)S(1)} all-gather(f32[144,128]{1,0:T(8,128)S(1)} %pad_maximum_fusion.own_ref), channel_id=2, replica_groups=mesh['xh'=2,'xl'=2,'zh'=4,'yh'=4,'yl'=2,'zl'=2,'core'=2] {'zl','core'}, dimensions={0}, use_global_device_ids=true | all-gather | bytes 368640 | tf_op jit(solution)/shard_map/all_gather | solution.py:124
  57.5 0.0 copy-done
  57.5 0.0 copy-done.1
  57.5 0.9 %shard_map.93 = (f32[48,128]{1,0:T(8,128)}, f32[48,128]{1,0:T(8,128)}, f32[48,128]{1,0:T(8,128)}, f32[144,128]{1,0:T(8,128)}) custom-call(s32[1,2]{1,0:T(1,128)S(1)} %copy-done, s32[1,6]{1,0:T(1,128)S(1)} %bitcast.20, f32[144,128]{1,0:T(8,128)S(1)} %pad_maximum_fusion.own_ref, f32[4,144,128]{2,1,0:T(8,128)S(1)} %bitcast.19), custom_call_target="tpu_custom_call" | custom-call | tf_op jit(solution)/shard_map/pallas_call | solution.py:126
  (3 shorter events, 0.1 us)
Async XLA Ops:
  24.1 27.3 %copy-start.2 = (f32[1,1,6144]{2,1,0:T(1,128)S(1)}, f32[1,1,6144]{2,1,0:T(1,128)}, u32[]{:S(2)}) copy-start(f32[1,1,6144]{2,1,0:T(1,128)} %param.7) | copy-start | bytes 73732
  24.1 27.3 %copy-start.3 = (f32[1,1,6144]{2,1,0:T(1,128)S(1)}, f32[1,1,6144]{2,1,0:T(1,128)}, u32[]{:S(2)}) copy-start(f32[1,1,6144]{2,1,0:T(1,128)} %param.8) | copy-start | bytes 73732
  24.1 27.3 %copy-start.4 = (f32[1,1,6144]{2,1,0:T(1,128)S(1)}, f32[1,1,6144]{2,1,0:T(1,128)}, u32[]{:S(2)}) copy-start(f32[1,1,6144]{2,1,0:T(1,128)} %param.9) | copy-start | bytes 73732
  24.2 33.3 %copy-start = (s32[1,2]{1,0:T(1,128)S(1)}, s32[1,2]{1,0:T(1,128)}, u32[]{:S(2)}) copy-start(s32[1,2]{1,0:T(1,128)} %holders_ref.1) | copy-start | bytes 28
  24.3 33.3 %copy-start.1 = (s32[6]{0:T(128)S(1)}, s32[6]{0:T(128)}, u32[]{:S(2)}) copy-start(s32[6]{0:T(128)} %param.11) | copy-start | bytes 76

commit v4 on v3

--- a/solution.py
+++ b/solution.py
@@ -18,6 +18,7 @@
 CODE = ("zl", "core")
 LANES = 128
 SCALE = 4096.0
+FIRST = 30
 
 
 def pairs(size, shifted):
@@ -47,14 +48,13 @@
         for yl in range(2):
             for zl in range(2):
                 for core in range(2):
-                    groups.append(
-                        [
-                            (((x * Z + z) * Y + y) * 2 + zl) * 2 + core
-                            for x in (2 + xl, xl)
-                            for z in reversed(range(Z))
-                            for y in (4 + yl, 6 + yl, yl, 2 + yl)
-                        ]
-                    )
+                    group = [
+                        (((x * Z + z) * Y + y) * 2 + zl) * 2 + core
+                        for x in range(xl, X, 2)
+                        for z in range(Z)
+                        for y in range(yl, Y, 2)
+                    ]
+                    groups.append(group[FIRST:] + group[:FIRST])
     return groups
 
 
@@ -96,12 +96,11 @@
     parts = lax.all_to_all(
         parts, DP + CODE, 0, 0, tiled=True, axis_index_groups=near_groups()
     )
-    summed = jnp.sum(parts.astype(jnp.float32), axis=0)
+    parts = jnp.concatenate([parts[:, FIRST:], parts[:, :FIRST]], axis=1).astype(jnp.float32)
+    summed = (parts[0] + parts[1]) + (parts[2] + parts[3])
     summed = (summed * SCALE).astype(jnp.float16)
-    pieces = summed.reshape(X // 2, Z, 2, Y // 4, rows, LANES)
-    pieces = lax.rev(pieces, (0, 1, 2)).reshape(summed.shape)
     summed = lax.all_to_all(
-        pieces, DP + CODE, 0, 0, tiled=True, axis_index_groups=far_groups()
+        summed, DP + CODE, 0, 0, tiled=True, axis_index_groups=far_groups()
     )
     gradient = jnp.sum(summed.astype(jnp.float32), axis=0) * (1.0 / SCALE)
 

time: 58.7 us -> 58.3 us (level)
  no operation moved by 1% of the time
where the time goes in v4:
time: 58.3 us; the launch traced here: 58 us
  blocking collectives  53.8 us (92%)
  local copies, waits for them, and re-layouts  2.08 us (4%)
  Pallas kernels  0.9 us (2%)
  between operations  0.76 us (1%)
    all_to_all x1, blocking collectives, local(): lax.all_to_all(summed, DP + CODE, 0, 0, tiled=True, axis_index_groups=far...  26.4 us
    all_to_all x1, blocking collectives, local(): lax.all_to_all(parts, DP + CODE, 0, 0, tiled=True, axis_index_groups=near...  21.3 us
    all_gather x1, blocking collectives, local(): states = lax.all_gather(own, CODE, axis=0, tiled=False)  6.04 us
    unnamed x11, local copies, waits for them, and re-layouts  1.78 us

profile of v4, /device:TPU:1, one launch (start us, length us, event | category | flops | bytes accessed | tf_op | source)
XLA Modules:
  0.0 58.0 jit_solution(12215833255416726844)
XLA Ops:
  0.6 1.8 %copy.14 = bf16[16,8,48,128]{3,2,1,0:T(8,128)(2,1)S(1)} copy(bf16[16,8,48,128]{3,1,2,0:T(8,128)(2,1)} %bitcast.23) | data formatting | bytes 3145728
  2.4 0.2 copy.12
  2.6 21.3 %all_to_all.10 = bf16[4,32,48,128]{3,2,1,0:T(8,128)(2,1)S(1)} all-to-all(bf16[4,32,48,128]{3,2,1,0:T(8,128)(2,1)S(1)} %bitcast.21), channel_id=1, replica_groups={{0,4,128,132},{8,12,136,140},{16,20,144,148},{24,28,152,156},{256,260,3..., dimensions={0} | all-to-all | bytes 3145728 | tf_op jit(solution)/shard_map/all_to_all | solution.py:96
  23.9 0.1 slice.25
  24.0 0.2 maximum_convert_fusion
  24.2 0.0 copy-start.2
  24.2 0.0 copy-start.3
  24.2 0.0 copy-start.4
  24.3 0.2 fusion.3
  24.5 0.0 copy-start
  24.5 0.0 copy-start.1
  24.5 26.4 %all_to_all.11 = f16[32,48,128]{2,1,0:T(8,128)(2,1)S(1)} all-to-all(f16[32,48,128]{2,1,0:T(8,128)(2,1)S(1)} %fusion.3), channel_id=1, replica_groups={{368,376,0,8,16,24,32,40,48,56,64,72,80,88,96,104,112,120,256,264,272,2..., dimensions={0} | all-to-all | bytes 786432 | tf_op jit(solution)/shard_map/all_to_all | solution.py:102
  50.9 0.1 convert_reduce_fusion
  51.0 0.0 copy-done.2
  51.0 0.0 copy-done.3
  51.0 0.0 copy-done.4
  51.1 6.0 %all-gather = f32[576,128]{1,0:T(8,128)S(1)} all-gather(f32[144,128]{1,0:T(8,128)S(1)} %pad_maximum_fusion.own_ref), channel_id=2, replica_groups=mesh['xh'=2,'xl'=2,'zh'=4,'yh'=4,'yl'=2,'zl'=2,'core'=2] {'zl','core'}, dimensions={0}, use_global_device_ids=true | all-gather | bytes 368640 | tf_op jit(solution)/shard_map/all_gather | solution.py:123
  57.1 0.0 copy-done
  57.1 0.0 copy-done.1
  57.1 0.9 %shard_map.93 = (f32[48,128]{1,0:T(8,128)}, f32[48,128]{1,0:T(8,128)}, f32[48,128]{1,0:T(8,128)}, f32[144,128]{1,0:T(8,128)}) custom-call(s32[1,2]{1,0:T(1,128)S(1)} %copy-done, s32[1,6]{1,0:T(1,128)S(1)} %bitcast.20, f32[144,128]{1,0:T(8,128)S(1)} %pad_maximum_fusion.own_ref, f32[4,144,128]{2,1,0:T(8,128)S(1)} %bitcast.19), custom_call_target="tpu_custom_call" | custom-call | tf_op jit(solution)/shard_map/pallas_call | solution.py:125
  (4 shorter events, 0.1 us)
Async XLA Ops:
  24.2 26.8 %copy-start.2 = (f32[1,1,6144]{2,1,0:T(1,128)S(1)}, f32[1,1,6144]{2,1,0:T(1,128)}, u32[]{:S(2)}) copy-start(f32[1,1,6144]{2,1,0:T(1,128)} %param.7) | copy-start | bytes 73732
  24.2 26.8 %copy-start.3 = (f32[1,1,6144]{2,1,0:T(1,128)S(1)}, f32[1,1,6144]{2,1,0:T(1,128)}, u32[]{:S(2)}) copy-start(f32[1,1,6144]{2,1,0:T(1,128)} %param.8) | copy-start | bytes 73732
  24.2 26.8 %copy-start.4 = (f32[1,1,6144]{2,1,0:T(1,128)S(1)}, f32[1,1,6144]{2,1,0:T(1,128)}, u32[]{:S(2)}) copy-start(f32[1,1,6144]{2,1,0:T(1,128)} %param.9) | copy-start | bytes 73732
  24.5 32.7 %copy-start = (s32[1,2]{1,0:T(1,128)S(1)}, s32[1,2]{1,0:T(1,128)}, u32[]{:S(2)}) copy-start(s32[1,2]{1,0:T(1,128)} %holders_ref.1) | copy-start | bytes 28
  24.5 32.7 %copy-start.1 = (s32[6]{0:T(128)S(1)}, s32[6]{0:T(128)}, u32[]{:S(2)}) copy-start(s32[6]{0:T(128)} %param.11) | copy-start | bytes 76

commit v5 on v4

--- a/solution.py
+++ b/solution.py
@@ -19,6 +19,7 @@
 LANES = 128
 SCALE = 4096.0
 FIRST = 30
+MEMBERS = (2, 3, 0, 1)
 
 
 def pairs(size, shifted):
@@ -73,12 +74,12 @@
     holders = holders_ref[...]
     nodes = nodes_ref[...].astype(jnp.float32)
     total = None
-    for i in range(states_ref.shape[0]):
+    for place, i in enumerate(MEMBERS):
         weight = jnp.zeros((1, 1), jnp.float32)
         for j in range(2):
             held = jnp.where(holders[:, j : j + 1] == member, 4.0, 0.0)
             weight += held / (nodes[:, j : j + 1] + nodes[:, 2 + i : 3 + i])
-        term = weight * states_ref[i]
+        term = weight * states_ref[place]
         total = term if total is None else total + term
     total_ref[...] = total
     copies.append(pltpu.make_async_copy(total_ref, parity_ref, sems.at[3]))
@@ -120,7 +121,10 @@
     new_params = params - learn_rate * update
 
     own = jnp.concatenate([new_params, new_moment, new_variance], axis=0)
-    states = lax.all_gather(own, CODE, axis=0, tiled=False)
+    code_groups = [[4 * shard + i for i in MEMBERS] for shard in range(X * Z * Y)]
+    states = lax.all_gather(
+        own, DP + CODE, axis=0, tiled=False, axis_index_groups=code_groups
+    )
     state = jax.ShapeDtypeStruct((rows, LANES), jnp.float32)
     new_params, new_moment, new_variance, parity = pl.pallas_call(
         finish_kernel,

time: 58.3 us -> 58.3 us (level)
  no operation moved by 1% of the time
where the time goes in v5:
time: 58.3 us; the launch traced here: 58 us
  blocking collectives  53.8 us (92%)
  local copies, waits for them, and re-layouts  2.08 us (4%)
  Pallas kernels  0.9 us (2%)
  between operations  0.76 us (1%)
    all_to_all x1, blocking collectives, local(): lax.all_to_all(summed, DP + CODE, 0, 0, tiled=True, axis_index_groups=far...  26.4 us
    all_to_all x1, blocking collectives, local(): lax.all_to_all(parts, DP + CODE, 0, 0, tiled=True, axis_index_groups=near...  21.3 us
    all_gather x1, blocking collectives, local(): lax.all_gather(own, DP + CODE, axis=0, tiled=False, axis_index_groups=cod...  6.04 us
    unnamed x11, local copies, waits for them, and re-layouts  1.78 us

profile of v5, /device:TPU:1, one launch (start us, length us, event | category | flops | bytes accessed | tf_op | source)
XLA Modules:
  0.0 58.0 jit_solution(5360570776730078821)
XLA Ops:
  0.6 1.8 %copy.14 = bf16[16,8,48,128]{3,2,1,0:T(8,128)(2,1)S(1)} copy(bf16[16,8,48,128]{3,1,2,0:T(8,128)(2,1)} %bitcast.23) | data formatting | bytes 3145728
  2.4 0.2 copy.12
  2.6 21.3 %all_to_all.10 = bf16[4,32,48,128]{3,2,1,0:T(8,128)(2,1)S(1)} all-to-all(bf16[4,32,48,128]{3,2,1,0:T(8,128)(2,1)S(1)} %bitcast.21), channel_id=1, replica_groups={{0,4,128,132},{8,12,136,140},{16,20,144,148},{24,28,152,156},{256,260,3..., dimensions={0} | all-to-all | bytes 3145728 | tf_op jit(solution)/shard_map/all_to_all | solution.py:97
  23.9 0.1 slice.25
  24.0 0.2 maximum_convert_fusion
  24.2 0.0 copy-start.2
  24.2 0.0 copy-start.3
  24.2 0.0 copy-start.4
  24.3 0.2 fusion.3
  24.5 0.0 copy-start
  24.5 0.0 copy-start.1
  24.5 26.4 %all_to_all.11 = f16[32,48,128]{2,1,0:T(8,128)(2,1)S(1)} all-to-all(f16[32,48,128]{2,1,0:T(8,128)(2,1)S(1)} %fusion.3), channel_id=1, replica_groups={{368,376,0,8,16,24,32,40,48,56,64,72,80,88,96,104,112,120,256,264,272,2..., dimensions={0} | all-to-all | bytes 786432 | tf_op jit(solution)/shard_map/all_to_all | solution.py:103
  50.9 0.1 convert_reduce_fusion
  51.0 0.0 copy-done.2
  51.0 0.0 copy-done.3
  51.0 0.0 copy-done.4
  51.1 6.0 %all-gather = f32[576,128]{1,0:T(8,128)S(1)} all-gather(f32[144,128]{1,0:T(8,128)S(1)} %pad_maximum_fusion.own_ref), channel_id=2, replica_groups={{2,3,0,1},{6,7,4,5},{10,11,8,9},{14,15,12,13},{18,19,16,17},{22,23,20,2..., dimensions={0}, use_global_device_ids=true | all-gather | bytes 368640 | tf_op jit(solution)/shard_map/all_gather | solution.py:125
  57.1 0.0 copy-done
  57.1 0.0 copy-done.1
  57.1 0.9 %shard_map.93 = (f32[48,128]{1,0:T(8,128)}, f32[48,128]{1,0:T(8,128)}, f32[48,128]{1,0:T(8,128)}, f32[144,128]{1,0:T(8,128)}) custom-call(s32[1,2]{1,0:T(1,128)S(1)} %copy-done, s32[1,6]{1,0:T(1,128)S(1)} %bitcast.20, f32[144,128]{1,0:T(8,128)S(1)} %pad_maximum_fusion.own_ref, f32[4,144,128]{2,1,0:T(8,128)S(1)} %bitcast.19), custom_call_target="tpu_custom_call" | custom-call | tf_op jit(solution)/shard_map/pallas_call | solution.py:129
  (4 shorter events, 0.1 us)
Async XLA Ops:
  24.2 26.8 %copy-start.2 = (f32[1,1,6144]{2,1,0:T(1,128)S(1)}, f32[1,1,6144]{2,1,0:T(1,128)}, u32[]{:S(2)}) copy-start(f32[1,1,6144]{2,1,0:T(1,128)} %param.7) | copy-start | bytes 73732
  24.2 26.8 %copy-start.3 = (f32[1,1,6144]{2,1,0:T(1,128)S(1)}, f32[1,1,6144]{2,1,0:T(1,128)}, u32[]{:S(2)}) copy-start(f32[1,1,6144]{2,1,0:T(1,128)} %param.8) | copy-start | bytes 73732
  24.2 26.8 %copy-start.4 = (f32[1,1,6144]{2,1,0:T(1,128)S(1)}, f32[1,1,6144]{2,1,0:T(1,128)}, u32[]{:S(2)}) copy-start(f32[1,1,6144]{2,1,0:T(1,128)} %param.9) | copy-start | bytes 73732
  24.5 32.7 %copy-start = (s32[1,2]{1,0:T(1,128)S(1)}, s32[1,2]{1,0:T(1,128)}, u32[]{:S(2)}) copy-start(s32[1,2]{1,0:T(1,128)} %holders_ref.1) | copy-start | bytes 28
  24.5 32.7 %copy-start.1 = (s32[6]{0:T(128)S(1)}, s32[6]{0:T(128)}, u32[]{:S(2)}) copy-start(s32[6]{0:T(128)} %param.11) | copy-start | bytes 76

commit v6 on v4

--- a/solution.py
+++ b/solution.py
@@ -96,9 +96,8 @@
     parts = lax.all_to_all(
         parts, DP + CODE, 0, 0, tiled=True, axis_index_groups=near_groups()
     )
-    parts = jnp.concatenate([parts[:, FIRST:], parts[:, :FIRST]], axis=1).astype(jnp.float32)
-    summed = (parts[0] + parts[1]) + (parts[2] + parts[3])
-    summed = (summed * SCALE).astype(jnp.float16)
+    summed = jnp.sum(parts.astype(jnp.float32), axis=0) * SCALE
+    summed = jnp.concatenate([summed[FIRST:], summed[:FIRST]], axis=0).astype(jnp.float16)
     summed = lax.all_to_all(
         summed, DP + CODE, 0, 0, tiled=True, axis_index_groups=far_groups()
     )

time: 58.3 us -> 58.3 us (level)
  no operation moved by 1% of the time
where the time goes in v6:
time: 58.3 us; the launch traced here: 58 us
  blocking collectives  53.8 us (92%)
  local copies, waits for them, and re-layouts  2.06 us (4%)
  Pallas kernels  0.9 us (2%)
  between operations  0.77 us (1%)
    all_to_all x1, blocking collectives, local(): lax.all_to_all(summed, DP + CODE, 0, 0, tiled=True, axis_index_groups=far...  26.4 us
    all_to_all x1, blocking collectives, local(): lax.all_to_all(parts, DP + CODE, 0, 0, tiled=True, axis_index_groups=near...  21.3 us
    all_gather x1, blocking collectives, local(): states = lax.all_gather(own, CODE, axis=0, tiled=False)  6.04 us
    unnamed x11, local copies, waits for them, and re-layouts  1.78 us

profile of v6, /device:TPU:1, one launch (start us, length us, event | category | flops | bytes accessed | tf_op | source)
XLA Modules:
  0.0 58.0 jit_solution(10750708823128859355)
XLA Ops:
  0.6 1.8 %copy.16 = bf16[16,8,48,128]{3,2,1,0:T(8,128)(2,1)S(1)} copy(bf16[16,8,48,128]{3,1,2,0:T(8,128)(2,1)} %bitcast.21) | data formatting | bytes 3145728
  2.4 0.2 copy.14
  2.6 21.3 %all_to_all.10 = bf16[4,32,48,128]{3,2,1,0:T(8,128)(2,1)S(1)} all-to-all(bf16[4,32,48,128]{3,2,1,0:T(8,128)(2,1)S(1)} %bitcast.19), channel_id=1, replica_groups={{0,4,128,132},{8,12,136,140},{16,20,144,148},{24,28,152,156},{256,260,3..., dimensions={0} | all-to-all | bytes 3145728 | tf_op jit(solution)/shard_map/all_to_all | solution.py:96
  23.9 0.2 convert_reduce_fusion
  24.1 0.1 multiply_convert_fusion
  24.2 0.0 copy-start.2
  24.2 0.0 copy-start.3
  24.2 0.0 copy-start.4
  24.3 0.0 copy-start
  24.3 0.0 copy-start.1
  24.3 0.1 slice.11
  24.4 0.1 pad_maximum_fusion
  24.5 26.4 %all_to_all.11 = f16[32,48,128]{2,1,0:T(8,128)(2,1)S(1)} all-to-all(f16[32,48,128]{2,1,0:T(8,128)(2,1)S(1)} %pad_maximum_fusion), channel_id=1, replica_groups={{368,376,0,8,16,24,32,40,48,56,64,72,80,88,96,104,112,120,256,264,272,2..., dimensions={0} | all-to-all | bytes 786432 | tf_op jit(solution)/shard_map/all_to_all | solution.py:101
  50.9 0.1 convert_reduce_fusion.1
  51.0 0.0 copy-done.2
  51.0 0.0 copy-done.3
  51.0 0.0 copy-done.4
  51.1 6.0 %all-gather = f32[576,128]{1,0:T(8,128)S(1)} all-gather(f32[144,128]{1,0:T(8,128)S(1)} %pad_maximum_fusion.1.own_ref), channel_id=2, replica_groups=mesh['xh'=2,'xl'=2,'zh'=4,'yh'=4,'yl'=2,'zl'=2,'core'=2] {'zl','core'}, dimensions={0}, use_global_device_ids=true | all-gather | bytes 368640 | tf_op jit(solution)/shard_map/all_gather | solution.py:122
  57.1 0.0 copy-done
  57.1 0.0 copy-done.1
  57.1 0.9 %shard_map.93 = (f32[48,128]{1,0:T(8,128)}, f32[48,128]{1,0:T(8,128)}, f32[48,128]{1,0:T(8,128)}, f32[144,128]{1,0:T(8,128)}) custom-call(s32[1,2]{1,0:T(1,128)S(1)} %copy-done, s32[1,6]{1,0:T(1,128)S(1)} %bitcast.18, f32[144,128]{1,0:T(8,128)S(1)} %pad_maximum_fusion.1.own_ref, f32[4,144,128]{2,1,0:T(8,128)S(1)} %bitcast.17), custom_call_target="tpu_custom_call" | custom-call | tf_op jit(solution)/shard_map/pallas_call | solution.py:124
  (4 shorter events, 0.1 us)
Async XLA Ops:
  24.2 26.8 %copy-start.2 = (f32[1,1,6144]{2,1,0:T(1,128)S(1)}, f32[1,1,6144]{2,1,0:T(1,128)}, u32[]{:S(2)}) copy-start(f32[1,1,6144]{2,1,0:T(1,128)} %param.7) | copy-start | bytes 73732
  24.2 26.8 %copy-start.3 = (f32[1,1,6144]{2,1,0:T(1,128)S(1)}, f32[1,1,6144]{2,1,0:T(1,128)}, u32[]{:S(2)}) copy-start(f32[1,1,6144]{2,1,0:T(1,128)} %param.8) | copy-start | bytes 73732
  24.2 26.8 %copy-start.4 = (f32[1,1,6144]{2,1,0:T(1,128)S(1)}, f32[1,1,6144]{2,1,0:T(1,128)}, u32[]{:S(2)}) copy-start(f32[1,1,6144]{2,1,0:T(1,128)} %param.9) | copy-start | bytes 73732
  24.3 32.9 %copy-start = (s32[1,2]{1,0:T(1,128)S(1)}, s32[1,2]{1,0:T(1,128)}, u32[]{:S(2)}) copy-start(s32[1,2]{1,0:T(1,128)} %holders_ref.1) | copy-start | bytes 28
  24.3 32.9 %copy-start.1 = (s32[6]{0:T(128)S(1)}, s32[6]{0:T(128)}, u32[]{:S(2)}) copy-start(s32[6]{0:T(128)} %param.11) | copy-start | bytes 76
